TPU v7x, 32 devices: a whole 2x2x4 slice. The times are simulated.
32 devices in a mesh: ctx: 16 (over z, x, core), tp: 2 (over y).
Axes of the slice: x: 2, y: 2, z: 4, core: 2. Of those that a mesh axis runs over, the one named last changes fastest.
Arguments:
- query_proj: bfloat16 [8192, 4096], P('ctx', 'tp'), may hold values from -6 to 6
- key_proj: bfloat16 [8192, 4096], P('ctx', 'tp'), may hold values from -6 to 6
- value_proj: bfloat16 [8192, 4096], P('ctx', 'tp'), may hold values from -6 to 6
- cotangent: bfloat16 [8192, 4096], P('ctx', 'tp'), may hold values from -6 to 6
- out_weight: bfloat16 [4096, 4096], P('tp'), may hold values from -0.09375 to 0.09375
- decay_rates: float32 [4096, 16], P('tp'), may hold values from 6.1035156e-05 to 0.1
- residues: float32 [4096, 16], P('tp'), may hold values from -1.8 to 1.8
- skip_gain: float32 [4096], P('tp'), may hold values from 0.5 to 1.5
Outputs:
- mixed: bfloat16 [8192, 4096], P('ctx', 'tp')
- grad_query: bfloat16 [8192, 4096], P('ctx', 'tp')
- grad_key: bfloat16 [8192, 4096], P('ctx', 'tp')
- grad_value: bfloat16 [8192, 4096], P('ctx', 'tp')
All inputs are finite; a program needn't handle non-finite values.
Results may differ from a plain program's by a relative error of at most 0.023.
Values may be sent and summed in bfloat16 or wider, within the bound.
A program may use at most 128 MiB of HBM per device.

v0:
```python
import functools

import jax
import jax.numpy as jnp
from jax import lax
from jax.experimental import pallas as pl
from jax.experimental.pallas import tpu as pltpu
from jax.sharding import PartitionSpec as P

SEGS = 8
LANES = 128
f32 = jnp.float32
bf16 = jnp.bfloat16
LIMIT = 56 * 1024 * 1024


def tree_sum(terms):
    while len(terms) > 1:
        pairs = [a + b for a, b in zip(terms[0::2], terms[1::2])]
        terms = pairs + ([terms[-1]] if len(terms) % 2 else [])
    return terms[0]


def rows_of(table):
    return [jnp.broadcast_to(table[m : m + 1], (SEGS, LANES)) for m in range(table.shape[0])]


def scan_segments(u_ref, y_ref, rates, amp, states, flipped):
    steps = u_ref.shape[0] // SEGS
    unroll = 8
    lam = rows_of(jnp.exp(-rates))
    gain = None if amp is None else rows_of(amp)

    def body(i, xs):
        for j in range(unroll):
            t = i * unroll + j
            if flipped:
                t = steps - 1 - t
            at = pl.ds(t, SEGS, stride=steps)
            u = u_ref[at, :]
            xs = [l * x + u for l, x in zip(lam, xs)]
            if gain is not None:
                y_ref[at, :] = tree_sum([g * x for g, x in zip(gain, xs)])
        return xs

    return lax.fori_loop(0, steps // unroll, body, states)


def local_ends(u_ref, rates, ends_ref, starts_ref, lanes, flipped):
    steps = u_ref.shape[0] // SEGS
    zero = jnp.zeros((SEGS, LANES), f32)
    ends = scan_segments(u_ref, None, rates, None, [zero] * rates.shape[0], flipped)
    place = lax.broadcasted_iota(jnp.int32, (SEGS, LANES), 0)

    def moved(x, by):
        if flipped:
            return jnp.where(place < SEGS - by, pltpu.roll(x, SEGS - by, 0), 0.0)
        return jnp.where(place >= by, pltpu.roll(x, by, 0), 0.0)

    factors = []
    by = 1
    while by < SEGS:
        factors.append((by, rows_of(jnp.exp(-rates * float(steps * by)))))
        by *= 2
    last = 0 if flipped else SEGS - 1
    for m, x in enumerate(ends):
        for by, factor in factors:
            x = x + factor[m] * moved(x, by)
        ends_ref[m : m + 1, lanes] = x[last : last + 1]
        starts_ref[m * SEGS : (m + 1) * SEGS, lanes] = moved(x, 1)


def full_scan(u_ref, y_ref, rates, amp, starts_ref, init, lanes, flipped):
    steps = u_ref.shape[0] // SEGS
    place = lax.broadcasted_iota(jnp.int32, (SEGS, LANES), 0)
    if flipped:
        place = SEGS - 1 - place
    past = place.astype(f32) * float(steps)
    states = []
    for m in range(rates.shape[0]):
        factor = jnp.exp(-rates[m : m + 1] * past)
        states.append(starts_ref[m * SEGS : (m + 1) * SEGS, lanes] + factor * init[m : m + 1])
    scan_segments(u_ref, y_ref, rates, amp, states, flipped)


def lane_groups(width):
    return [slice(g * LANES, (g + 1) * LANES) for g in range(width // LANES)]


def forward_ends_kernel(k_ref, v_ref, rates_ref, ends_ref, starts_ref, u_ref):
    for lanes in lane_groups(k_ref.shape[1]):
        gated = k_ref[:, lanes].astype(f32) * v_ref[:, lanes].astype(f32)
        u_ref[...] = gated.astype(bf16).astype(f32)
        local_ends(u_ref, rates_ref[:, lanes], ends_ref, starts_ref, lanes, False)


def forward_kernel(
    q_ref, k_ref, v_ref, rates_ref, amp_ref, skip_ref, starts_ref, init_ref,
    out_ref, summed_ref, u_ref, y_ref,
):
    for lanes in lane_groups(k_ref.shape[1]):
        gated = k_ref[:, lanes].astype(f32) * v_ref[:, lanes].astype(f32)
        u_ref[...] = gated.astype(bf16).astype(f32)
        full_scan(
            u_ref, y_ref, rates_ref[:, lanes], amp_ref[:, lanes], starts_ref,
            init_ref[:, lanes], lanes, False,
        )
        conv = y_ref[...].astype(bf16).astype(f32)
        summed = conv + skip_ref[:, lanes] * u_ref[...]
        summed_ref[:, lanes] = summed.astype(bf16)
        out_ref[:, lanes] = (q_ref[:, lanes].astype(f32) * summed).astype(bf16)


def matmul_kernel(at_ref, x_ref, w_ref, out_ref):
    out_ref[...] = jnp.dot(x_ref[...], w_ref[...], preferred_element_type=f32).astype(bf16)


def grad_kernel(n_tp, at_ref, *refs):
    cots, weights = refs[:n_tp], refs[n_tp : 2 * n_tp]
    q_ref, summed_ref, rates_ref = refs[2 * n_tp : 2 * n_tp + 3]
    grad_query_ref, grad_conv_ref, ends_ref, starts_ref, u_ref = refs[2 * n_tp + 3 :]
    grad_in = sum(
        lax.dot_general(
            c_ref[...], w_ref[...], (((1,), (1,)), ((), ())), preferred_element_type=f32
        )
        for c_ref, w_ref in zip(cots, weights)
    )
    grad_query_ref[...] = (grad_in * summed_ref[...].astype(f32)).astype(bf16)
    grad_conv_ref[...] = (grad_in * q_ref[...].astype(f32)).astype(bf16)
    for lanes in lane_groups(q_ref.shape[1]):
        u_ref[...] = grad_conv_ref[:, lanes].astype(f32)
        local_ends(u_ref, rates_ref[:, lanes], ends_ref, starts_ref, lanes, True)


def backward_kernel(
    g_ref, k_ref, v_ref, rates_ref, amp_ref, skip_ref, starts_ref, init_ref,
    grad_key_ref, grad_value_ref, u_ref, y_ref,
):
    for lanes in lane_groups(k_ref.shape[1]):
        u_ref[...] = g_ref[:, lanes].astype(f32)
        full_scan(
            u_ref, y_ref, rates_ref[:, lanes], amp_ref[:, lanes], starts_ref,
            init_ref[:, lanes], lanes, True,
        )
        back = y_ref[...].astype(bf16).astype(f32)
        grad = back + skip_ref[:, lanes] * u_ref[...]
        grad_key_ref[:, lanes] = (grad * v_ref[:, lanes].astype(f32)).astype(bf16)
        grad_value_ref[:, lanes] = (grad * k_ref[:, lanes].astype(f32)).astype(bf16)


def across_devices(ends, rates, length, flipped):
    count = lax.axis_size("ctx")
    modes, channels = ends.shape
    rows = modes * channels // LANES

    def spread(x):
        return x.reshape(modes, channels // LANES, LANES).reshape(rows, LANES)

    mine = lax.all_to_all(
        spread(ends).reshape(count, rows // count, LANES), "ctx", split_axis=0, concat_axis=0
    )
    width = rows // count
    my_rates = lax.dynamic_slice_in_dim(spread(rates), lax.axis_index("ctx") * width, width, 0)
    factor = jnp.exp(-my_rates * float(length))
    state = jnp.zeros_like(mine[0])
    before = [None] * count
    for place in reversed(range(count)) if flipped else range(count):
        before[place] = state
        state = factor * state + mine[place]
    back = lax.all_to_all(jnp.stack(before), "ctx", split_axis=0, concat_axis=0)
    return back.reshape(modes, channels)


def per_device(q, k, v, cot, weight, decay_rates, residues, skip_gain):
    length, channels = q.shape
    modes = decay_rates.shape[1]
    n_tp = lax.axis_size("tp")
    me = lax.axis_index("tp").astype(jnp.int32)
    shared = cot.shape[1]

    others = [
        lax.ppermute(cot, "tp", [((i + s) % n_tp, i) for i in range(n_tp)])
        for s in range(1, n_tp)
    ]

    rates = decay_rates.T
    amp = (residues * jnp.sqrt(-jnp.expm1(-2.0 * decay_rates))).T
    skip = skip_gain.reshape(1, channels)

    block = 256
    steps = channels // block
    wide = pl.BlockSpec((length, block), lambda i: (0, i))
    table = pl.BlockSpec((modes, block), lambda i: (0, i))
    starts_spec = pl.BlockSpec((modes * SEGS, block), lambda i: (0, i))
    line = pl.BlockSpec((1, block), lambda i: (0, i))
    params = pltpu.CompilerParams(vmem_limit_bytes=LIMIT)
    signal = jax.ShapeDtypeStruct((length, channels), bf16)
    ends_shape = jax.ShapeDtypeStruct((modes, channels), f32)
    starts_shape = jax.ShapeDtypeStruct((modes * SEGS, channels), f32)
    scratch = pltpu.VMEM((length, LANES), f32)
    cell = length * channels * modes

    ends, starts = pl.pallas_call(
        forward_ends_kernel,
        grid=(steps,),
        in_specs=[wide, wide, table],
        out_specs=[table, starts_spec],
        out_shape=[ends_shape, starts_shape],
        scratch_shapes=[scratch],
        compiler_params=params,
        cost_estimate=pl.CostEstimate(
            flops=2 * cell, bytes_accessed=length * channels * 6, transcendentals=0
        ),
        name="forward_ends",
    )(k, v, rates)
    init = across_devices(ends, rates, length, False)
    output_in, summed = pl.pallas_call(
        forward_kernel,
        grid=(steps,),
        in_specs=[wide, wide, wide, table, table, line, starts_spec, table],
        out_specs=[wide, wide],
        out_shape=[signal, signal],
        scratch_shapes=[scratch, scratch],
        compiler_params=params,
        cost_estimate=pl.CostEstimate(
            flops=4 * cell, bytes_accessed=length * channels * 12, transcendentals=0
        ),
        name="forward_scan",
    )(q, k, v, rates, amp, skip, starts, init)

    cols = 512
    per_target = shared // cols

    def project(target):
        return pl.pallas_call(
            matmul_kernel,
            grid_spec=pltpu.PrefetchScalarGridSpec(
                num_scalar_prefetch=1,
                grid=(per_target,),
                in_specs=[
                    pl.BlockSpec((length, channels), lambda i, at: (0, 0)),
                    pl.BlockSpec((channels, cols), lambda i, at: (0, at[0] * per_target + i)),
                ],
                out_specs=pl.BlockSpec((length, cols), lambda i, at: (0, i)),
            ),
            out_shape=jax.ShapeDtypeStruct((length, shared), bf16),
            compiler_params=params,
            cost_estimate=pl.CostEstimate(
                flops=2 * length * channels * shared,
                bytes_accessed=2 * (channels * shared + length * (channels + shared)),
                transcendentals=0,
            ),
            name="project",
        )(target.reshape(1), output_in, weight)

    received = [
        lax.ppermute(
            project(lax.rem(me + s, n_tp)), "tp", [(i, (i + s) % n_tp) for i in range(n_tp)]
        )
        for s in range(1, n_tp)
    ]

    def weight_spec(s):
        return pl.BlockSpec((block, shared), lambda i, at: (i, lax.rem(at[0] + s, n_tp)))

    def with_at(spec):
        return pl.BlockSpec(spec.block_shape, lambda i, at: (0, i))

    grad_query, grad_conv, back_ends, back_starts = pl.pallas_call(
        functools.partial(grad_kernel, n_tp),
        grid_spec=pltpu.PrefetchScalarGridSpec(
            num_scalar_prefetch=1,
            grid=(steps,),
            in_specs=[pl.BlockSpec((length, shared), lambda i, at: (0, 0))] * n_tp
            + [weight_spec(s) for s in range(n_tp)]
            + [with_at(wide), with_at(wide), with_at(table)],
            out_specs=[with_at(wide), with_at(wide), with_at(table), with_at(starts_spec)],
            scratch_shapes=[scratch],
        ),
        out_shape=[signal, signal, ends_shape, starts_shape],
        compiler_params=params,
        cost_estimate=pl.CostEstimate(
            flops=2 * length * channels * shared * n_tp,
            bytes_accessed=2 * n_tp * shared * channels + length * channels * 8,
            transcendentals=0,
        ),
        name="grad_projection",
    )(me.reshape(1), cot, *others, *([weight] * n_tp), q, summed, rates)
    own = project(me)
    back_init = across_devices(back_ends, rates, length, True)
    grad_key, grad_value = pl.pallas_call(
        backward_kernel,
        grid=(steps,),
        in_specs=[wide, wide, wide, table, table, line, starts_spec, table],
        out_specs=[wide, wide],
        out_shape=[signal, signal],
        scratch_shapes=[scratch, scratch],
        compiler_params=params,
        cost_estimate=pl.CostEstimate(
            flops=4 * cell, bytes_accessed=length * channels * 12, transcendentals=0
        ),
        name="backward_scan",
    )(grad_conv, k, v, rates, amp, skip, back_starts, back_init)

    mixed = own.astype(f32)
    for part in received:
        mixed = mixed + part.astype(f32)
    return (mixed.astype(bf16), grad_query, grad_key, grad_value)


def solution(mesh):
    spread = P("ctx", "tp")
    by_tp = P("tp", None)
    return jax.shard_map(
        per_device,
        mesh=mesh,
        in_specs=(spread, spread, spread, spread, by_tp, by_tp, by_tp, P("tp")),
        out_specs=(spread, spread, spread, spread),
        check_vma=False,
    )
```

profile of v0, /device:TPU:0, one launch (start us, length us, event | category | flops | bytes accessed | tf_op | source)
XLA Modules:
  0.0 159.4 jit_solution(11707420864674545860)
XLA Ops:
  0.7 10.2 %forward_ends.1 = (f32[16,2048]{1,0:T(8,128)}, f32[128,2048]{1,0:T(8,128)}) custom-call(bf16[512,2048]{1,0:T(8,128)(2,1)} %k_ref.5, bf16[512,2048]{1,0:T(8,128)(2,1)} %v_ref.5, f32[16,2048]{1,0:T(8,128)} %bitcast.330), custom_call_target="tpu_custom_call" | custom-call | flops 33554432 | bytes 6291456 | tf_op jit(solution)/shard_map/forward_ends/pallas_call | solution.py:203
  10.8 1.6 copy.12
  12.4 7.4 %all-to-all-start = ((f32[16,16,128]{2,1,0:T(8,128)}), f32[16,16,128]{2,1,0:T(8,128)S(1)}, u32[]{:S(2)}, u32[]{:S(2)}) async-start(f32[16,16,128]{2,1,0:T(8,128)} %bitcast.66), calls=%async_computation | async-start | bytes 262144 | tf_op jit(solution)/shard_map/all_to_all | solution.py:159
  19.8 1.6 collective-permute-start.1
  22.0 5.7 %all-to-all-done = f32[16,16,128]{2,1,0:T(8,128)S(1)} async-done(((f32[16,16,128]{2,1,0:T(8,128)}), f32[16,16,128]{2,1,0:T(8,128)S(1)}, u32[]{:S(2)}, u32[]{:S(2)}) %all-to-all-start) | async-done | bytes 131104 | tf_op jit(solution)/shard_map/all_to_all | solution.py:159
  28.9 0.6 constant_dynamic-update-slice_fusion.12
  29.5 0.6 constant_dynamic-update-slice_fusion.11
  30.8 0.6 constant_dynamic-update-slice_fusion.9
  32.0 0.6 constant_dynamic-update-slice_fusion.7
  33.2 0.6 constant_dynamic-update-slice_fusion.5
  35.7 0.6 constant_dynamic-update-slice_fusion.1
  36.3 0.6 constant_dynamic-update-slice_fusion
  36.9 3.5 %all-to-all-start.1 = ((f32[16,16,128]{2,1,0:T(8,128)}), f32[16,16,128]{2,1,0:T(8,128)S(1)}, u32[]{:S(2)}, u32[]{:S(2)}) async-start(f32[16,16,128]{2,1,0:T(8,128)} %constant_dynamic-update-slice_fusion), calls=%async_computation.1 | async-start | bytes 262144 | tf_op jit(solution)/shard_map/all_to_all | solution.py:170
  40.4 0.7 multiply_bitcast_fusion.amp_ref
  41.2 7.2 %all-to-all-done.1 = f32[16,16,128]{2,1,0:T(8,128)S(1)} async-done(((f32[16,16,128]{2,1,0:T(8,128)}), f32[16,16,128]{2,1,0:T(8,128)S(1)}, u32[]{:S(2)}, u32[]{:S(2)}) %all-to-all-start.1) | async-done | bytes 131104 | tf_op jit(solution)/shard_map/all_to_all | solution.py:170
  48.3 0.7 copy.19
  49.0 16.7 %forward_scan.1 = (bf16[512,2048]{1,0:T(8,128)(2,1)}, bf16[512,2048]{1,0:T(8,128)(2,1)}) custom-call(bf16[512,2048]{1,0:T(8,128)(2,1)} %refs_4_.1, bf16[512,2048]{1,0:T(8,128)(2,1)} %k_ref.5, bf16[512,2048]{1,0:T(8,128)(2,1)} %v_ref.5, f32[16,2048]{1,0:T(8,128)} %bitcast.331, f32[16,2048]{1,0:T(8,128)} %multiply_bitcast_fusion.amp_ref, f32[1,2048]{1,0:T(1,128)} %bitcast.341, ...), custom_call_target="tpu_custom_call" | custom-call | flops 67108864 | bytes 12582912 | tf_op jit(solution)/shard_map/forward_scan/pallas_call | solution.py:217
  65.7 2.2 %collective-permute-done.1.refs_1_ = bf16[512,2048]{1,0:T(8,128)(2,1)} collective-permute-done((bf16[512,2048]{1,0:T(8,128)(2,1)S(1)}, bf16[512,2048]{1,0:T(8,128)(2,1)}, u32[]{:S(2)}, u32[]{:S(2)}) %collective-permute-start.1) | collective-permute-done | bytes 2097184 | tf_op jit(solution)/shard_map/ppermute | solution.py:182
  67.9 23.3 %grad_projection.1 = (bf16[512,2048]{1,0:T(8,128)(2,1)}, bf16[512,2048]{1,0:T(8,128)(2,1)}, f32[16,2048]{1,0:T(8,128)}, f32[128,2048]{1,0:T(8,128)}) custom-call(s32[1]{0:T(128)} %bitcast.at_ref, bf16[512,2048]{1,0:T(8,128)(2,1)} %refs_0_.1, bf16[512,2048]{1,0:T(8,128)(2,1)} %collective-permute-done.1.refs_1_, bf16[2048,4096]{1,0:T(8,128)(2,1)} %refs_3_.1, ...), custom_call_target="tpu_custom_call" | custom-call | flops 8589934592 | bytes 25165824 | tf_op jit(solution)/shard_map/grad_projection/pallas_call | solution.py:269
  91.2 1.6 copy.14
  92.8 5.7 %all-to-all-start.2 = ((f32[16,16,128]{2,1,0:T(8,128)}), f32[16,16,128]{2,1,0:T(8,128)S(1)}, u32[]{:S(2)}, u32[]{:S(2)}) async-start(f32[16,16,128]{2,1,0:T(8,128)} %bitcast.70), calls=%async_computation.2 | async-start | bytes 262144 | tf_op jit(solution)/shard_map/all_to_all | solution.py:159
  98.5 8.8 %project.3 = bf16[512,2048]{1,0:T(8,128)(2,1)} custom-call(s32[1]{0:T(128)} %bitcast.34.at_ref, bf16[512,2048]{1,0:T(8,128)(2,1)} %get-tuple-element.16.x_ref, bf16[2048,4096]{1,0:T(8,128)(2,1)} %refs_3_.1), custom_call_target="tpu_custom_call" | custom-call | flops 4294967296 | bytes 12582912 | tf_op jit(solution)/shard_map/project/pallas_call | solution.py:235
  107.3 1.5 collective-permute-start
  108.8 0.6 constant_dynamic-update-slice_fusion.31
  109.5 0.6 constant_dynamic-update-slice_fusion.30
  116.1 0.6 constant_dynamic-update-slice_fusion.19
  118.6 6.0 %all-to-all-start.3 = ((f32[16,16,128]{2,1,0:T(8,128)}), f32[16,16,128]{2,1,0:T(8,128)S(1)}, u32[]{:S(2)}, u32[]{:S(2)}) async-start(f32[16,16,128]{2,1,0:T(8,128)} %constant_dynamic-update-slice_fusion.16), calls=%async_computation.3 | async-start | bytes 262144 | tf_op jit(solution)/shard_map/all_to_all | solution.py:170
  124.6 8.8 %project.2 = bf16[512,2048]{1,0:T(8,128)(2,1)} custom-call(s32[1]{0:T(128)} %bitcast.at_ref, bf16[512,2048]{1,0:T(8,128)(2,1)} %get-tuple-element.16.x_ref, bf16[2048,4096]{1,0:T(8,128)(2,1)} %refs_3_.1), custom_call_target="tpu_custom_call" | custom-call | flops 4294967296 | bytes 12582912 | tf_op jit(solution)/shard_map/project/pallas_call | solution.py:235
  133.4 0.7 copy.18
  134.0 18.3 %backward_scan.1 = (bf16[512,2048]{1,0:T(8,128)(2,1)}, bf16[512,2048]{1,0:T(8,128)(2,1)}) custom-call(bf16[512,2048]{1,0:T(8,128)(2,1)} %get-tuple-element.19.g_ref, bf16[512,2048]{1,0:T(8,128)(2,1)} %k_ref.5, bf16[512,2048]{1,0:T(8,128)(2,1)} %v_ref.5, f32[16,2048]{1,0:T(8,128)} %bitcast.333, f32[16,2048]{1,0:T(8,128)} %multiply_bitcast_fusion.amp_ref, ...), custom_call_target="tpu_custom_call" | custom-call | flops 67108864 | bytes 12582912 | tf_op jit(solution)/shard_map/backward_scan/pallas_call | solution.py:291
  152.4 3.2 %collective-permute-done = bf16[512,2048]{1,0:T(8,128)(2,1)} collective-permute-done((bf16[512,2048]{1,0:T(8,128)(2,1)}, bf16[512,2048]{1,0:T(8,128)(2,1)}, u32[]{:S(2)}, u32[]{:S(2)}) %collective-permute-start) | collective-permute-done | bytes 2097184 | tf_op jit(solution)/shard_map/ppermute | solution.py:257
  155.6 3.8 %add_convert_fusion = bf16[512,2048]{1,0:T(8,128)(2,1)} fusion(bf16[512,2048]{1,0:T(8,128)(2,1)} %collective-permute-done, bf16[512,2048]{1,0:T(8,128)(2,1)S(1)} %copy-done), kind=kLoop, calls=%fused_computation | loop fusion | flops 4194304 | bytes 6291456 | tf_op jit(solution)/shard_map/convert_element_type | solution.py:308
  (33 shorter events, 13.4 us)
Async XLA Ops:
  0.6 19.1 %copy-start.2 = (bf16[512,2048]{1,0:T(8,128)(2,1)S(1)}, bf16[512,2048]{1,0:T(8,128)(2,1)}, u32[]{:S(2)}) copy-start(bf16[512,2048]{1,0:T(8,128)(2,1)} %refs_0_.1) | copy-start | bytes 6291460
  0.6 20.7 %copy-start.1 = (f32[2048,16]{0,1:T(8,128)S(1)}, f32[2048,16]{0,1:T(8,128)}, u32[]{:S(2)}) copy-start(f32[2048,16]{0,1:T(8,128)} %param.13) | copy-start | bytes 393220
  0.7 39.8 %copy-start.3 = (f32[2048,16]{0,1:T(8,128)S(1)}, f32[2048,16]{0,1:T(8,128)}, u32[]{:S(2)}) copy-start(f32[2048,16]{0,1:T(8,128)} %param.14) | copy-start | bytes 393220
  12.4 15.3 %all-to-all-start = ((f32[16,16,128]{2,1,0:T(8,128)}), f32[16,16,128]{2,1,0:T(8,128)S(1)}, u32[]{:S(2)}, u32[]{:S(2)}) async-start(f32[16,16,128]{2,1,0:T(8,128)} %bitcast.66), calls=%async_computation | async-start | bytes 262144 | tf_op jit(solution)/shard_map/all_to_all | solution.py:159
  19.8 48.1 %collective-permute-start.1 = (bf16[512,2048]{1,0:T(8,128)(2,1)S(1)}, bf16[512,2048]{1,0:T(8,128)(2,1)}, u32[]{:S(2)}, u32[]{:S(2)}) collective-permute-start(bf16[512,2048]{1,0:T(8,128)(2,1)S(1)} %copy-done.2), channel_id=1, source_target_pairs={{1,0},{0,1},{3,2},{2,3},{5,4},{4,5},{7,6},{6,7},{9,8},{8,9},{11,10... | collective-permute-start | bytes 6291464 | tf_op jit(solution)/shard_map/ppermute | solution.py:182
  36.9 11.4 %all-to-all-start.1 = ((f32[16,16,128]{2,1,0:T(8,128)}), f32[16,16,128]{2,1,0:T(8,128)S(1)}, u32[]{:S(2)}, u32[]{:S(2)}) async-start(f32[16,16,128]{2,1,0:T(8,128)} %constant_dynamic-update-slice_fusion), calls=%async_computation.1 | async-start | bytes 262144 | tf_op jit(solution)/shard_map/all_to_all | solution.py:170
  92.8 16.0 %all-to-all-start.2 = ((f32[16,16,128]{2,1,0:T(8,128)}), f32[16,16,128]{2,1,0:T(8,128)S(1)}, u32[]{:S(2)}, u32[]{:S(2)}) async-start(f32[16,16,128]{2,1,0:T(8,128)} %bitcast.70), calls=%async_computation.2 | async-start | bytes 262144 | tf_op jit(solution)/shard_map/all_to_all | solution.py:159
  107.3 48.3 %collective-permute-start = (bf16[512,2048]{1,0:T(8,128)(2,1)}, bf16[512,2048]{1,0:T(8,128)(2,1)}, u32[]{:S(2)}, u32[]{:S(2)}) collective-permute-start(bf16[512,2048]{1,0:T(8,128)(2,1)} %project.3), channel_id=1, source_target_pairs={{0,1},{1,0},{2,3},{3,2},{4,5},{5,4},{6,7},{7,6},{8,9},{9,8},{10,11... | collective-permute-start | bytes 6291464 | tf_op jit(solution)/shard_map/ppermute | solution.py:257
  118.6 14.8 %all-to-all-start.3 = ((f32[16,16,128]{2,1,0:T(8,128)}), f32[16,16,128]{2,1,0:T(8,128)S(1)}, u32[]{:S(2)}, u32[]{:S(2)}) async-start(f32[16,16,128]{2,1,0:T(8,128)} %constant_dynamic-update-slice_fusion.16), calls=%async_computation.3 | async-start | bytes 262144 | tf_op jit(solution)/shard_map/all_to_all | solution.py:170
  134.0 21.5 %copy-start = (bf16[512,2048]{1,0:T(8,128)(2,1)S(1)}, bf16[512,2048]{1,0:T(8,128)(2,1)}, u32[]{:S(2)}) copy-start(bf16[512,2048]{1,0:T(8,128)(2,1)} %project.2) | copy-start | bytes 6291460
where the time goes:
time: 160 us; the launch traced here: 159 us
  Pallas kernels  86 us (54%)
  starting transfers between devices  25.7 us (16%)
  other arithmetic  19.9 us (12%)
  waiting for transfers between devices  18.3 us (11%)
  local copies, waits for them, and re-layouts  8.79 us (5%)
    pallas_call x1, Pallas kernels, per_device(): pl.pallas_call(functools.partial(grad_kernel, n_tp), grid_spec=pltpu.Pref...  23.3 us
    pallas_call x1, Pallas kernels, per_device(): pl.pallas_call(backward_kernel, grid=(steps,), in_specs=[wide, wide, wide...  18.3 us
    pallas_call x2, Pallas kernels, project(): pl.pallas_call(matmul_kernel, grid_spec=pltpu.PrefetchScalarGridSpec(num_...  17.5 us
    pallas_call x1, Pallas kernels, per_device(): pl.pallas_call(forward_kernel, grid=(steps,), in_specs=[wide, wide, wide,...  16.7 us
    unnamed x24, other arithmetic  14.7 us
    all_to_all x2, starting transfers between devices, across_devices(): lax.all_to_all(spread(ends).reshape(count, rows // count, LANES), 'ctx',...  13.1 us
    pallas_call x1, Pallas kernels, per_device(): pl.pallas_call(forward_ends_kernel, grid=(steps,), in_specs=[wide, wide,...  10.2 us
    all_to_all x2, starting transfers between devices, across_devices(): back = lax.all_to_all(jnp.stack(before), 'ctx', split_axis=0, concat_axis=0)  9.51 us
  transfers between devices with their start and end apart: 6, of which 4 were waited for; matrix products, arithmetic and copies ran while one was open for 14% of the time, Pallas kernels for 33%

commit v1 on v0

v1 whole, which is shorter than its diff:
```python
import functools

import jax
import jax.numpy as jnp
from jax import lax
from jax.experimental import pallas as pl
from jax.experimental.pallas import tpu as pltpu
from jax.sharding import PartitionSpec as P

SEGS = 8
LANES = 128
GAP = 8
f32 = jnp.float32
bf16 = jnp.bfloat16
LIMIT = 56 * 1024 * 1024
LIGHT = pl.CostEstimate(flops=0, bytes_accessed=0, transcendentals=0)


def tree_sum(terms):
    while len(terms) > 1:
        pairs = [a + b for a, b in zip(terms[0::2], terms[1::2])]
        terms = pairs + ([terms[-1]] if len(terms) % 2 else [])
    return terms[0]


def rows_of(table):
    return [jnp.broadcast_to(table[m : m + 1], (SEGS, LANES)) for m in range(table.shape[0])]


def put_segments(ref, value):
    steps = value.shape[0] // SEGS
    for s in range(SEGS):
        ref[s * (steps + GAP) : s * (steps + GAP) + steps] = value[s * steps : (s + 1) * steps]


def get_segments(ref):
    steps = ref.shape[0] // SEGS - GAP
    return jnp.concatenate(
        [ref[s * (steps + GAP) : s * (steps + GAP) + steps] for s in range(SEGS)], axis=0
    )


def step_rows(steps, t, flipped):
    return pl.ds(steps - 1 - t if flipped else t, SEGS, stride=steps + GAP)


def scan_ends(u_ref, rates, flipped):
    steps = u_ref.shape[0] // SEGS - GAP
    half = steps // 2
    unroll = 8
    lam = rows_of(jnp.exp(-rates))

    def body(i, carry):
        early, late = carry
        for j in range(unroll):
            t = i * unroll + j
            u = u_ref[step_rows(steps, t, flipped), :]
            w = u_ref[step_rows(steps, t + half, flipped), :]
            early = [l * x + u for l, x in zip(lam, early)]
            late = [l * x + w for l, x in zip(lam, late)]
        return early, late

    zero = [jnp.zeros((SEGS, LANES), f32)] * rates.shape[0]
    early, late = lax.fori_loop(0, half // unroll, body, (zero, zero))
    factor = rows_of(jnp.exp(-rates * float(half)))
    return [f * x + y for f, x, y in zip(factor, early, late)]


def scan_signal(u_ref, y_ref, rates, amp, states, flipped):
    steps = u_ref.shape[0] // SEGS - GAP
    unroll = 8
    lam = rows_of(jnp.exp(-rates))
    gain = rows_of(amp)

    def body(i, xs):
        for j in range(unroll):
            at = step_rows(steps, i * unroll + j, flipped)
            u = u_ref[at, :]
            xs = [l * x + u for l, x in zip(lam, xs)]
            y_ref[at, :] = tree_sum([g * x for g, x in zip(gain, xs)])
        return xs

    lax.fori_loop(0, steps // unroll, body, states)


def local_ends(u_ref, rates, ends_ref, starts_ref, lanes, rows, flipped):
    steps = u_ref.shape[0] // SEGS - GAP
    ends = scan_ends(u_ref, rates, flipped)
    place = lax.broadcasted_iota(jnp.int32, (SEGS, LANES), 0)

    def moved(x, by):
        if flipped:
            return jnp.where(place < SEGS - by, pltpu.roll(x, SEGS - by, 0), 0.0)
        return jnp.where(place >= by, pltpu.roll(x, by, 0), 0.0)

    factors = []
    by = 1
    while by < SEGS:
        factors.append((by, rows_of(jnp.exp(-rates * float(steps * by)))))
        by *= 2
    last = 0 if flipped else SEGS - 1
    for m, x in enumerate(ends):
        for by, factor in factors:
            x = x + factor[m] * moved(x, by)
        ends_ref[rows.start + m : rows.start + m + 1] = x[last : last + 1]
        starts_ref[m * SEGS : (m + 1) * SEGS, lanes] = moved(x, 1)


def full_scan(u_ref, y_ref, rates, amp, starts_ref, init, lanes, flipped):
    steps = u_ref.shape[0] // SEGS - GAP
    place = lax.broadcasted_iota(jnp.int32, (SEGS, LANES), 0)
    if flipped:
        place = SEGS - 1 - place
    past = place.astype(f32) * float(steps)
    states = []
    for m in range(rates.shape[0]):
        factor = jnp.exp(-rates[m : m + 1] * past)
        states.append(starts_ref[m * SEGS : (m + 1) * SEGS, lanes] + factor * init[m : m + 1])
    scan_signal(u_ref, y_ref, rates, amp, states, flipped)


def lane_groups(width, modes):
    return [
        (slice(g * LANES, (g + 1) * LANES), slice(g * modes, (g + 1) * modes))
        for g in range(width // LANES)
    ]


def groups_of(signal_ref, table_ref):
    width = signal_ref.shape[1]
    return lane_groups(width, table_ref.shape[0] * LANES // width)


def forward_ends_kernel(k_ref, v_ref, rates_ref, ends_ref, starts_ref, u_ref):
    for lanes, rows in groups_of(k_ref, rates_ref):
        gated = k_ref[:, lanes].astype(f32) * v_ref[:, lanes].astype(f32)
        gated = gated.astype(bf16).astype(f32)
        put_segments(u_ref, gated)
        local_ends(u_ref, rates_ref[rows], ends_ref, starts_ref, lanes, rows, False)


def forward_kernel(
    q_ref, k_ref, v_ref, rates_ref, amp_ref, skip_ref, starts_ref, init_ref,
    out_ref, summed_ref, u_ref, y_ref,
):
    for lanes, rows in groups_of(k_ref, rates_ref):
        gated = k_ref[:, lanes].astype(f32) * v_ref[:, lanes].astype(f32)
        gated = gated.astype(bf16).astype(f32)
        put_segments(u_ref, gated)
        full_scan(
            u_ref, y_ref, rates_ref[rows], amp_ref[rows], starts_ref,
            init_ref[rows], lanes, False,
        )
        conv = get_segments(y_ref).astype(bf16).astype(f32)
        summed = conv + skip_ref[:, lanes] * get_segments(u_ref)
        summed_ref[:, lanes] = summed.astype(bf16)
        out_ref[:, lanes] = (q_ref[:, lanes].astype(f32) * summed).astype(bf16)


def matmul_kernel(at_ref, x_ref, w_ref, out_ref):
    out_ref[...] = jnp.dot(x_ref[...], w_ref[...], preferred_element_type=f32).astype(bf16)


def grad_kernel(n_tp, at_ref, *refs):
    cots, weights = refs[:n_tp], refs[n_tp : 2 * n_tp]
    q_ref, summed_ref, rates_ref = refs[2 * n_tp : 2 * n_tp + 3]
    grad_query_ref, grad_conv_ref, ends_ref, starts_ref, u_ref = refs[2 * n_tp + 3 :]
    grad_in = sum(
        lax.dot_general(
            c_ref[...], w_ref[...], (((1,), (1,)), ((), ())), preferred_element_type=f32
        )
        for c_ref, w_ref in zip(cots, weights)
    )
    grad_query_ref[...] = (grad_in * summed_ref[...].astype(f32)).astype(bf16)
    grad_conv_ref[...] = (grad_in * q_ref[...].astype(f32)).astype(bf16)
    for lanes, rows in groups_of(q_ref, rates_ref):
        put_segments(u_ref, grad_conv_ref[:, lanes].astype(f32))
        local_ends(u_ref, rates_ref[rows], ends_ref, starts_ref, lanes, rows, True)


def backward_kernel(
    g_ref, k_ref, v_ref, rates_ref, amp_ref, skip_ref, starts_ref, init_ref,
    grad_key_ref, grad_value_ref, u_ref, y_ref,
):
    for lanes, rows in groups_of(k_ref, rates_ref):
        put_segments(u_ref, g_ref[:, lanes].astype(f32))
        full_scan(
            u_ref, y_ref, rates_ref[rows], amp_ref[rows], starts_ref,
            init_ref[rows], lanes, True,
        )
        back = get_segments(y_ref).astype(bf16).astype(f32)
        grad = back + skip_ref[:, lanes] * get_segments(u_ref)
        grad_key_ref[:, lanes] = (grad * v_ref[:, lanes].astype(f32)).astype(bf16)
        grad_value_ref[:, lanes] = (grad * k_ref[:, lanes].astype(f32)).astype(bf16)


def exchange_kernel(
    length, flipped, ends_ref, rates_ref, init_ref,
    mine_ref, before_ref, back_ref, send_out, recv_out, send_back, recv_back,
):
    count = ends_ref.shape[0]
    me, row = lax.axis_index("ctx"), lax.axis_index("tp")
    partners = [lax.rem(me + p, count) for p in range(1, count)]

    barrier = pltpu.get_barrier_semaphore()
    for to in partners:
        pl.semaphore_signal(
            barrier, inc=1, device_id=(to, row), device_id_type=pl.DeviceIdType.MESH
        )
    pl.semaphore_wait(barrier, count - 1)

    def send(src_ref, dst_ref, sent, arrived):
        copies = [
            pltpu.make_async_remote_copy(
                src_ref=src_ref.at[to],
                dst_ref=dst_ref.at[me],
                send_sem=sent.at[p],
                recv_sem=arrived.at[p],
                device_id=(to, row),
                device_id_type=pl.DeviceIdType.MESH,
            )
            for p, to in enumerate(partners)
        ]
        for copy in copies:
            copy.start()
        return copies

    outward = send(ends_ref, mine_ref, send_out, recv_out)
    mine_ref[me] = ends_ref[me]
    factor = jnp.exp(-rates_ref[me] * float(length))
    for copy in outward:
        copy.wait_recv()
    state = jnp.zeros_like(factor)
    for place in reversed(range(count)) if flipped else range(count):
        before_ref[place] = state
        state = factor * state + mine_ref[place]
    homeward = send(before_ref, back_ref, send_back, recv_back)
    back_ref[me] = before_ref[me]
    for copy in homeward:
        copy.wait_recv()
    init_ref[...] = back_ref[...]
    for copy in outward + homeward:
        copy.wait_send()


def across_devices(ends, rates, length, flipped):
    count = lax.axis_size("ctx")
    rows = ends.shape[0]
    shape = (count, rows // count, LANES)
    whole = pl.BlockSpec(memory_space=pltpu.VMEM)
    init = pl.pallas_call(
        functools.partial(exchange_kernel, length, flipped),
        out_shape=jax.ShapeDtypeStruct(shape, f32),
        in_specs=[whole, whole],
        out_specs=whole,
        scratch_shapes=[pltpu.VMEM(shape, f32)] * 3
        + [pltpu.SemaphoreType.DMA((count - 1,))] * 4,
        compiler_params=pltpu.CompilerParams(
            collective_id=1 if flipped else 0, has_side_effects=True
        ),
        cost_estimate=LIGHT,
        name="exchange_back" if flipped else "exchange_forward",
    )(ends.reshape(shape), rates.reshape(shape))
    return init.reshape(rows, LANES)


def per_device(q, k, v, cot, weight, decay_rates, residues, skip_gain):
    length, channels = q.shape
    modes = decay_rates.shape[1]
    n_tp = lax.axis_size("tp")
    me = lax.axis_index("tp").astype(jnp.int32)
    shared = cot.shape[1]

    others = [
        lax.ppermute(cot, "tp", [((i + s) % n_tp, i) for i in range(n_tp)])
        for s in range(1, n_tp)
    ]

    def by_group(x):
        x = jnp.transpose(x.reshape(channels // LANES, LANES, modes), (0, 2, 1))
        return x.reshape(channels // LANES * modes, LANES)

    rates = by_group(decay_rates)
    amp = by_group(residues * jnp.sqrt(-jnp.expm1(-2.0 * decay_rates)))
    skip = skip_gain.reshape(1, channels)

    block = 256
    steps = channels // block
    wide = pl.BlockSpec((length, block), lambda i: (0, i))
    table = pl.BlockSpec((block // LANES * modes, LANES), lambda i: (i, 0))
    starts_spec = pl.BlockSpec((modes * SEGS, block), lambda i: (0, i))
    line = pl.BlockSpec((1, block), lambda i: (0, i))
    params = pltpu.CompilerParams(vmem_limit_bytes=LIMIT)
    signal = jax.ShapeDtypeStruct((length, channels), bf16)
    ends_shape = jax.ShapeDtypeStruct((channels // LANES * modes, LANES), f32)
    starts_shape = jax.ShapeDtypeStruct((modes * SEGS, channels), f32)
    scratch = pltpu.VMEM((length + SEGS * GAP, LANES), f32)

    ends, starts = pl.pallas_call(
        forward_ends_kernel,
        grid=(steps,),
        in_specs=[wide, wide, table],
        out_specs=[table, starts_spec],
        out_shape=[ends_shape, starts_shape],
        scratch_shapes=[scratch],
        compiler_params=params,
        cost_estimate=LIGHT,
        name="forward_ends",
    )(k, v, rates)
    init = across_devices(ends, rates, length, False)
    output_in, summed = pl.pallas_call(
        forward_kernel,
        grid=(steps,),
        in_specs=[wide, wide, wide, table, table, line, starts_spec, table],
        out_specs=[wide, wide],
        out_shape=[signal, signal],
        scratch_shapes=[scratch, scratch],
        compiler_params=params,
        cost_estimate=LIGHT,
        name="forward_scan",
    )(q, k, v, rates, amp, skip, starts, init)

    cols = 512
    per_target = shared // cols

    def project(target):
        return pl.pallas_call(
            matmul_kernel,
            grid_spec=pltpu.PrefetchScalarGridSpec(
                num_scalar_prefetch=1,
                grid=(per_target,),
                in_specs=[
                    pl.BlockSpec((length, channels), lambda i, at: (0, 0)),
                    pl.BlockSpec((channels, cols), lambda i, at: (0, at[0] * per_target + i)),
                ],
                out_specs=pl.BlockSpec((length, cols), lambda i, at: (0, i)),
            ),
            out_shape=jax.ShapeDtypeStruct((length, shared), bf16),
            compiler_params=params,
            cost_estimate=LIGHT,
            name="project",
        )(target.reshape(1), output_in, weight)

    parts = [project(lax.rem(me + s, n_tp)) for s in range(1, n_tp)]
    others, parts = lax.optimization_barrier((others, parts))
    received = [
        lax.ppermute(part, "tp", [(i, (i + s) % n_tp) for i in range(n_tp)])
        for s, part in enumerate(parts, 1)
    ]

    def weight_spec(s):
        return pl.BlockSpec((block, shared), lambda i, at: (i, lax.rem(at[0] + s, n_tp)))

    def with_at(spec):
        return pl.BlockSpec(spec.block_shape, lambda i, at: spec.index_map(i))

    grad_query, grad_conv, back_ends, back_starts = pl.pallas_call(
        functools.partial(grad_kernel, n_tp),
        grid_spec=pltpu.PrefetchScalarGridSpec(
            num_scalar_prefetch=1,
            grid=(steps,),
            in_specs=[pl.BlockSpec((length, shared), lambda i, at: (0, 0))] * n_tp
            + [weight_spec(s) for s in range(n_tp)]
            + [with_at(wide), with_at(wide), with_at(table)],
            out_specs=[with_at(wide), with_at(wide), with_at(table), with_at(starts_spec)],
            scratch_shapes=[scratch],
        ),
        out_shape=[signal, signal, ends_shape, starts_shape],
        compiler_params=params,
        cost_estimate=LIGHT,
        name="grad_projection",
    )(me.reshape(1), cot, *others, *([weight] * n_tp), q, summed, rates)
    own = project(me)
    back_init = across_devices(back_ends, rates, length, True)
    grad_key, grad_value = pl.pallas_call(
        backward_kernel,
        grid=(steps,),
        in_specs=[wide, wide, wide, table, table, line, starts_spec, table],
        out_specs=[wide, wide],
        out_shape=[signal, signal],
        scratch_shapes=[scratch, scratch],
        compiler_params=params,
        cost_estimate=LIGHT,
        name="backward_scan",
    )(grad_conv, k, v, rates, amp, skip, back_starts, back_init)

    mixed = own.astype(f32)
    for part in received:
        mixed = mixed + part.astype(f32)
    return (mixed.astype(bf16), grad_query, grad_key, grad_value)


def solution(mesh):
    spread = P("ctx", "tp")
    by_tp = P("tp", None)
    return jax.shard_map(
        per_device,
        mesh=mesh,
        in_specs=(spread, spread, spread, spread, by_tp, by_tp, by_tp, P("tp")),
        out_specs=(spread, spread, spread, spread),
        check_vma=False,
    )
```

time: 160 us -> 118 us (0.74)
  starting transfers between devices: 25.7 us -> 3.54 us
  Pallas kernels: 86 us -> 107 us
  waiting for transfers between devices: 18.3 us -> 0.01 us
  other arithmetic: 19.9 us -> 4.54 us
  local copies, waits for them, and re-layouts: 8.79 us -> 1.64 us
    pallas_call x0 -> x2, Pallas kernels: none -> 30.3 us  [across_devices(): pl.pallas_call(functools.partial(exchange_kernel, length, flipped), out_s...]
    all_to_all x4 -> x0, starting transfers between devices: 22.6 us -> none  [the longest x2 13.1 us: across_devices(): lax.all_to_all(spread(ends).reshape(count, rows // count, LANES), 'ctx',...]
    unnamed x24 -> x0, other arithmetic: 14.7 us -> none
    all_to_all x4 -> x0, waiting for transfers between devices: 12.9 us -> none  [the longest x2 7.16 us: across_devices(): back = lax.all_to_all(jnp.stack(before), 'ctx', split_axis=0, concat_axis=0)]
    unnamed x18 -> x8, local copies, waits for them, and re-layouts: 8.16 us -> 0.02 us
    pallas_call x1, Pallas kernels: 18.3 us -> 14 us  [per_device(): pl.pallas_call(backward_kernel, grid=(steps,), in_specs=[wide, wide, wide...]
    ppermute x1, waiting for transfers between devices: 3.2 us -> 0.01 us  [per_device(): lax.ppermute(part, 'tp', [(i, (i + s) % n_tp) for i in range(n_tp)])]
    pallas_call x1, Pallas kernels: 16.7 us -> 14.1 us  [per_device(): pl.pallas_call(forward_kernel, grid=(steps,), in_specs=[wide, wide, wide,...]
  transfers between devices with their start and end apart: 6 -> 2, of which waited for: 4 -> 0; matrix products, arithmetic and copies ran while one was open for 14% -> 2% of each run, Pallas kernels for 33% -> 91%
where the time goes in v1:
time: 118 us
  Pallas kernels  107 us (91%)
  other arithmetic  4.54 us (4%)
  starting transfers between devices  3.54 us (3%)
  local copies, waits for them, and re-layouts  1.64 us (1%)
    pallas_call x2, Pallas kernels, across_devices(): pl.pallas_call(functools.partial(exchange_kernel, length, flipped), out_s...  30.3 us
    pallas_call x1, Pallas kernels, per_device(): pl.pallas_call(functools.partial(grad_kernel, n_tp), grid_spec=pltpu.Pref...  21.9 us
    pallas_call x2, Pallas kernels, project(): pl.pallas_call(matmul_kernel, grid_spec=pltpu.PrefetchScalarGridSpec(num_...  17.7 us
    pallas_call x1, Pallas kernels, per_device(): pl.pallas_call(forward_kernel, grid=(steps,), in_specs=[wide, wide, wide,...  14.1 us
    pallas_call x1, Pallas kernels, per_device(): pl.pallas_call(backward_kernel, grid=(steps,), in_specs=[wide, wide, wide...  14 us
    pallas_call x1, Pallas kernels, per_device(): pl.pallas_call(forward_ends_kernel, grid=(steps,), in_specs=[wide, wide,...  9.42 us
    convert_element_type x1, other arithmetic, per_device(): return (mixed.astype(bf16), grad_query, grad_key, grad_value)  3.81 us
    ppermute x1, starting transfers between devices, per_device(): lax.ppermute(cot, 'tp', [((i + s) % n_tp, i) for i in range(n_tp)])  3.03 us
  transfers between devices with their start and end apart: 2, of which 0 were waited for; matrix products, arithmetic and copies ran while one was open for 2% of the time, Pallas kernels for 91%

profile of v1, /device:TPU:0, one launch (start us, length us, event | category | flops | bytes accessed | tf_op | source)
XLA Modules:
  0.0 117.8 jit_solution(13652597204200066008)
XLA Ops:
  0.6 3.0 %collective-permute-start = (bf16[512,2048]{1,0:T(8,128)(2,1)}, bf16[512,2048]{1,0:T(8,128)(2,1)S(1)}, u32[]{:S(2)}, u32[]{:S(2)}) collective-permute-start(bf16[512,2048]{1,0:T(8,128)(2,1)} %refs_0_.1), channel_id=1, source_target_pairs={{1,0},{0,1},{3,2},{2,3},{5,4},{4,5},{7,6},{6,7},{9,8},{8,9},{11,10... | collective-permute-start | bytes 6291464 | tf_op jit(solution)/shard_map/ppermute | solution.py:275
  3.7 1.6 %fusion = (f32[16,16,128]{2,1,0:T(8,128)}, f32[16,128,16]{1,2,0:T(8,128)}) fusion(f32[2048,16]{0,1:T(8,128)} %param.13), kind=kLoop, calls=%fused_computation.4 | loop fusion | bytes 393216 | tf_op jit(solution)/shard_map/transpose | solution.py:280
  5.3 0.0 copy-start.2
  5.3 0.0 copy-start.3
  5.3 9.4 %forward_ends.1 = (f32[256,128]{1,0:T(8,128)}, f32[128,2048]{1,0:T(8,128)}) custom-call(bf16[512,2048]{1,0:T(8,128)(2,1)} %k_ref.5, bf16[512,2048]{1,0:T(8,128)(2,1)} %v_ref.5, f32[256,128]{1,0:T(8,128)} %bitcast.26), custom_call_target="tpu_custom_call" | custom-call | tf_op jit(solution)/shard_map/forward_ends/pallas_call | solution.py:299
  14.7 16.3 %exchange_forward.1 = f32[16,16,128]{2,1,0:T(8,128)} custom-call(f32[16,16,128]{2,1,0:T(8,128)} %bitcast.35, f32[16,16,128]{2,1,0:T(8,128)} %get-tuple-element.28.rates_ref), custom_call_target="tpu_custom_call" | custom-call | tf_op jit(solution)/shard_map/exchange_forward/pallas_call | solution.py:251
  31.0 0.0 copy-done.2
  31.0 0.0 copy-done.3
  31.0 0.7 copy_bitcast_fusion
  31.8 14.1 %forward_scan.1 = (bf16[512,2048]{1,0:T(8,128)(2,1)}, bf16[512,2048]{1,0:T(8,128)(2,1)}) custom-call(bf16[512,2048]{1,0:T(8,128)(2,1)} %refs_4_.1, bf16[512,2048]{1,0:T(8,128)(2,1)} %k_ref.5, bf16[512,2048]{1,0:T(8,128)(2,1)} %v_ref.5, f32[256,128]{1,0:T(8,128)} %bitcast.27, f32[256,128]{1,0:T(8,128)} %bitcast.30, f32[1,2048]{1,0:T(1,128)} %bitcast.36, ...), custom_call_target="tpu_custom_call" | custom-call | tf_op jit(solution)/shard_map/forward_scan/pallas_call | solution.py:311
  45.9 8.7 %project.3 = bf16[512,2048]{1,0:T(8,128)(2,1)} custom-call(s32[1]{0:T(128)} %bitcast.9.at_ref, bf16[512,2048]{1,0:T(8,128)(2,1)} %get-tuple-element.18.x_ref, bf16[2048,4096]{1,0:T(8,128)(2,1)} %refs_3_.1), custom_call_target="tpu_custom_call" | custom-call | tf_op jit(solution)/shard_map/project/pallas_call | solution.py:327
  54.6 0.0 collective-permute-done.refs_1_
  54.6 0.0 copy-start.1
  54.6 0.5 collective-permute-start.1
  55.1 9.0 %project.2 = bf16[512,2048]{1,0:T(8,128)(2,1)} custom-call(s32[1]{0:T(128)} %bitcast.at_ref, bf16[512,2048]{1,0:T(8,128)(2,1)} %get-tuple-element.18.x_ref, bf16[2048,4096]{1,0:T(8,128)(2,1)} %refs_3_.1), custom_call_target="tpu_custom_call" | custom-call | tf_op jit(solution)/shard_map/project/pallas_call | solution.py:327
  64.1 0.0 copy-done.1
  64.1 21.9 %grad_projection.1 = (bf16[512,2048]{1,0:T(8,128)(2,1)}, bf16[512,2048]{1,0:T(8,128)(2,1)}, f32[256,128]{1,0:T(8,128)}, f32[128,2048]{1,0:T(8,128)}) custom-call(s32[1]{0:T(128)} %bitcast.at_ref, bf16[512,2048]{1,0:T(8,128)(2,1)} %refs_0_.1, bf16[512,2048]{1,0:T(8,128)(2,1)} %copy-done.1, bf16[2048,4096]{1,0:T(8,128)(2,1)} %refs_3_.1, ...), custom_call_target="tpu_custom_call" | custom-call | tf_op jit(solution)/shard_map/grad_projection/pallas_call | solution.py:357
  86.0 14.0 %exchange_back.1 = f32[16,16,128]{2,1,0:T(8,128)} custom-call(f32[16,16,128]{2,1,0:T(8,128)} %bitcast.34, f32[16,16,128]{2,1,0:T(8,128)} %get-tuple-element.28.rates_ref), custom_call_target="tpu_custom_call" | custom-call | tf_op jit(solution)/shard_map/exchange_back/pallas_call | solution.py:251
  100.0 0.0 copy-start
  100.0 14.0 %backward_scan.1 = (bf16[512,2048]{1,0:T(8,128)(2,1)}, bf16[512,2048]{1,0:T(8,128)(2,1)}) custom-call(bf16[512,2048]{1,0:T(8,128)(2,1)} %get-tuple-element.23.g_ref, bf16[512,2048]{1,0:T(8,128)(2,1)} %k_ref.5, bf16[512,2048]{1,0:T(8,128)(2,1)} %v_ref.5, f32[256,128]{1,0:T(8,128)} %bitcast.29, f32[256,128]{1,0:T(8,128)} %bitcast.31, f32[1,2048]{1,0:T(1,128)} %bitcast.37, ...), custom_call_target="tpu_custom_call" | custom-call | tf_op jit(solution)/shard_map/backward_scan/pallas_call | solution.py:375
  114.0 0.0 collective-permute-done.1
  114.0 0.0 copy-done
  114.0 3.8 %add_convert_fusion = bf16[512,2048]{1,0:T(8,128)(2,1)} fusion(bf16[512,2048]{1,0:T(8,128)(2,1)} %collective-permute-done.1, bf16[512,2048]{1,0:T(8,128)(2,1)S(1)} %copy-done), kind=kLoop, calls=%fused_computation | loop fusion | flops 4194304 | bytes 6291456 | tf_op jit(solution)/shard_map/convert_element_type | solution.py:390
Async XLA Ops:
  0.6 54.0 %collective-permute-start = (bf16[512,2048]{1,0:T(8,128)(2,1)}, bf16[512,2048]{1,0:T(8,128)(2,1)S(1)}, u32[]{:S(2)}, u32[]{:S(2)}) collective-permute-start(bf16[512,2048]{1,0:T(8,128)(2,1)} %refs_0_.1), channel_id=1, source_target_pairs={{1,0},{0,1},{3,2},{2,3},{5,4},{4,5},{7,6},{6,7},{9,8},{8,9},{11,10... | collective-permute-start | bytes 6291464 | tf_op jit(solution)/shard_map/ppermute | solution.py:275
  5.3 25.7 %copy-start.2 = (f32[2048,16]{0,1:T(8,128)S(1)}, f32[2048,16]{0,1:T(8,128)}, u32[]{:S(2)}) copy-start(f32[2048,16]{0,1:T(8,128)} %param.13) | copy-start | bytes 393220
  5.3 25.7 %copy-start.3 = (f32[2048,16]{0,1:T(8,128)S(1)}, f32[2048,16]{0,1:T(8,128)}, u32[]{:S(2)}) copy-start(f32[2048,16]{0,1:T(8,128)} %param.14) | copy-start | bytes 393220
  54.6 9.5 %copy-start.1 = (bf16[512,2048]{1,0:T(8,128)(2,1)}, bf16[512,2048]{1,0:T(8,128)(2,1)S(1)}, u32[]{:S(2)}) copy-start(bf16[512,2048]{1,0:T(8,128)(2,1)S(1)} %collective-permute-done.refs_1_) | copy-start | bytes 6291460
  54.6 59.4 %collective-permute-start.1 = (bf16[512,2048]{1,0:T(8,128)(2,1)}, bf16[512,2048]{1,0:T(8,128)(2,1)}, u32[]{:S(2)}, u32[]{:S(2)}) collective-permute-start(bf16[512,2048]{1,0:T(8,128)(2,1)} %project.3), channel_id=1, source_target_pairs={{0,1},{1,0},{2,3},{3,2},{4,5},{5,4},{6,7},{7,6},{8,9},{9,8},{10,11... | collective-permute-start | bytes 6291464 | tf_op jit(solution)/shard_map/ppermute | solution.py:347
  100.0 14.0 %copy-start = (bf16[512,2048]{1,0:T(8,128)(2,1)S(1)}, bf16[512,2048]{1,0:T(8,128)(2,1)}, u32[]{:S(2)}) copy-start(bf16[512,2048]{1,0:T(8,128)(2,1)} %project.2) | copy-start | bytes 6291460

commit v2 on v1

--- a/solution.py
+++ b/solution.py
@@ -179,9 +179,10 @@
 
 
 def backward_kernel(
-    g_ref, k_ref, v_ref, rates_ref, amp_ref, skip_ref, starts_ref, init_ref,
-    grad_key_ref, grad_value_ref, u_ref, y_ref,
+    g_ref, k_ref, v_ref, rates_ref, amp_ref, skip_ref, starts_ref, init_ref, *refs
 ):
+    *part_refs, grad_key_ref, grad_value_ref, mixed_ref, u_ref, y_ref = refs
+    mixed_ref[...] = sum(part_ref[...].astype(f32) for part_ref in part_refs).astype(bf16)
     for lanes, rows in groups_of(k_ref, rates_ref):
         put_segments(u_ref, g_ref[:, lanes].astype(f32))
         full_scan(
@@ -372,22 +373,20 @@
     )(me.reshape(1), cot, *others, *([weight] * n_tp), q, summed, rates)
     own = project(me)
     back_init = across_devices(back_ends, rates, length, True)
-    grad_key, grad_value = pl.pallas_call(
+    grad_key, grad_value, mixed = pl.pallas_call(
         backward_kernel,
         grid=(steps,),
-        in_specs=[wide, wide, wide, table, table, line, starts_spec, table],
-        out_specs=[wide, wide],
-        out_shape=[signal, signal],
+        in_specs=[wide, wide, wide, table, table, line, starts_spec, table]
+        + [wide] * n_tp,
+        out_specs=[wide, wide, wide],
+        out_shape=[signal, signal, signal],
         scratch_shapes=[scratch, scratch],
         compiler_params=params,
         cost_estimate=LIGHT,
         name="backward_scan",
-    )(grad_conv, k, v, rates, amp, skip, back_starts, back_init)
-
-    mixed = own.astype(f32)
-    for part in received:
-        mixed = mixed + part.astype(f32)
-    return (mixed.astype(bf16), grad_query, grad_key, grad_value)
+    )(grad_conv, k, v, rates, amp, skip, back_starts, back_init, own, *received)
+
+    return (mixed, grad_query, grad_key, grad_value)
 
 
 def solution(mesh):

time: 118 us -> 118 us (level)
  other arithmetic: 4.54 us -> 0.75 us
  waiting for transfers between devices: 0.01 us -> 2.45 us
    convert_element_type x1 -> x0, other arithmetic: 3.81 us -> none  [per_device(): return (mixed.astype(bf16), grad_query, grad_key, grad_value)]
    ppermute x1, waiting for transfers between devices: 0.01 us -> 2.45 us  [per_device(): lax.ppermute(part, 'tp', [(i, (i + s) % n_tp) for i in range(n_tp)])]
  transfers between devices with their start and end apart: 2 -> 2, of which waited for: 0 -> 1; matrix products, arithmetic and copies ran while one was open for 2% -> 2% of each run, Pallas kernels for 91% -> 80%
where the time goes in v2:
time: 118 us; the launch traced here: 117 us
  Pallas kernels  108 us (92%)
  starting transfers between devices  3.54 us (3%)
  waiting for transfers between devices  2.45 us (2%)
  local copies, waits for them, and re-layouts  1.63 us (1%)
    pallas_call x2, Pallas kernels, across_devices(): pl.pallas_call(functools.partial(exchange_kernel, length, flipped), out_s...  30.3 us
    pallas_call x1, Pallas kernels, per_device(): pl.pallas_call(functools.partial(grad_kernel, n_tp), grid_spec=pltpu.Pref...  21.9 us
    pallas_call x2, Pallas kernels, project(): pl.pallas_call(matmul_kernel, grid_spec=pltpu.PrefetchScalarGridSpec(num_...  17.8 us
    pallas_call x1, Pallas kernels, per_device(): pl.pallas_call(backward_kernel, grid=(steps,), in_specs=[wide, wide, wide...  14.8 us
    pallas_call x1, Pallas kernels, per_device(): pl.pallas_call(forward_kernel, grid=(steps,), in_specs=[wide, wide, wide,...  14.1 us
    pallas_call x1, Pallas kernels, per_device(): pl.pallas_call(forward_ends_kernel, grid=(steps,), in_specs=[wide, wide,...  9.42 us
    ppermute x1, starting transfers between devices, per_device(): lax.ppermute(cot, 'tp', [((i + s) % n_tp, i) for i in range(n_tp)])  3.03 us
    ppermute x1, waiting for transfers between devices, per_device(): lax.ppermute(part, 'tp', [(i, (i + s) % n_tp) for i in range(n_tp)])  2.45 us
  transfers between devices with their start and end apart: 2, of which 1 were waited for; matrix products, arithmetic and copies ran while one was open for 2% of the time, Pallas kernels for 80%

profile of v2, /device:TPU:0, one launch (start us, length us, event | category | flops | bytes accessed | tf_op | source)
XLA Modules:
  0.0 117.4 jit_solution(7337349182444489720)
XLA Ops:
  0.6 3.0 %collective-permute-start = (bf16[512,2048]{1,0:T(8,128)(2,1)}, bf16[512,2048]{1,0:T(8,128)(2,1)S(1)}, u32[]{:S(2)}, u32[]{:S(2)}) collective-permute-start(bf16[512,2048]{1,0:T(8,128)(2,1)} %refs_0_.1), channel_id=1, source_target_pairs={{1,0},{0,1},{3,2},{2,3},{5,4},{4,5},{7,6},{6,7},{9,8},{8,9},{11,10... | collective-permute-start | bytes 6291464 | tf_op jit(solution)/shard_map/ppermute | solution.py:276
  3.7 1.6 %fusion = (f32[16,16,128]{2,1,0:T(8,128)}, f32[16,128,16]{1,2,0:T(8,128)}) fusion(f32[2048,16]{0,1:T(8,128)} %param.13), kind=kLoop, calls=%fused_computation.3 | loop fusion | bytes 393216 | tf_op jit(solution)/shard_map/transpose | solution.py:281
  5.3 0.0 copy-start.1
  5.3 0.0 copy-start.2
  5.3 9.4 %forward_ends.1 = (f32[256,128]{1,0:T(8,128)}, f32[128,2048]{1,0:T(8,128)}) custom-call(bf16[512,2048]{1,0:T(8,128)(2,1)} %k_ref.5, bf16[512,2048]{1,0:T(8,128)(2,1)} %v_ref.5, f32[256,128]{1,0:T(8,128)} %bitcast.26), custom_call_target="tpu_custom_call" | custom-call | tf_op jit(solution)/shard_map/forward_ends/pallas_call | solution.py:300
  14.7 16.3 %exchange_forward.1 = f32[16,16,128]{2,1,0:T(8,128)} custom-call(f32[16,16,128]{2,1,0:T(8,128)} %bitcast.35, f32[16,16,128]{2,1,0:T(8,128)} %get-tuple-element.30.rates_ref), custom_call_target="tpu_custom_call" | custom-call | tf_op jit(solution)/shard_map/exchange_forward/pallas_call | solution.py:252
  31.0 0.0 copy-done.1
  31.0 0.0 copy-done.2
  31.0 0.7 copy_bitcast_fusion
  31.8 14.1 %forward_scan.1 = (bf16[512,2048]{1,0:T(8,128)(2,1)}, bf16[512,2048]{1,0:T(8,128)(2,1)}) custom-call(bf16[512,2048]{1,0:T(8,128)(2,1)} %refs_4_.1, bf16[512,2048]{1,0:T(8,128)(2,1)} %k_ref.5, bf16[512,2048]{1,0:T(8,128)(2,1)} %v_ref.5, f32[256,128]{1,0:T(8,128)} %bitcast.27, f32[256,128]{1,0:T(8,128)} %bitcast.30, f32[1,2048]{1,0:T(1,128)} %bitcast.36, ...), custom_call_target="tpu_custom_call" | custom-call | tf_op jit(solution)/shard_map/forward_scan/pallas_call | solution.py:312
  45.9 8.8 %project.2 = bf16[512,2048]{1,0:T(8,128)(2,1)} custom-call(s32[1]{0:T(128)} %bitcast.1.at_ref, bf16[512,2048]{1,0:T(8,128)(2,1)} %get-tuple-element.19.x_ref, bf16[2048,4096]{1,0:T(8,128)(2,1)} %w_ref.3), custom_call_target="tpu_custom_call" | custom-call | tf_op jit(solution)/shard_map/project/pallas_call | solution.py:328
  54.7 0.0 collective-permute-done.refs_1_
  54.7 0.0 copy-start
  54.7 0.5 collective-permute-start.1
  55.2 9.0 %project.3.refs_0_ = bf16[512,2048]{1,0:T(8,128)(2,1)} custom-call(s32[1]{0:T(128)} %bitcast.at_ref, bf16[512,2048]{1,0:T(8,128)(2,1)} %get-tuple-element.19.x_ref, bf16[2048,4096]{1,0:T(8,128)(2,1)} %w_ref.3), custom_call_target="tpu_custom_call" | custom-call | tf_op jit(solution)/shard_map/project/pallas_call | solution.py:328
  64.2 0.0 copy-done
  64.2 21.9 %grad_projection.1 = (bf16[512,2048]{1,0:T(8,128)(2,1)}, bf16[512,2048]{1,0:T(8,128)(2,1)}, f32[256,128]{1,0:T(8,128)}, f32[128,2048]{1,0:T(8,128)}) custom-call(s32[1]{0:T(128)} %bitcast.at_ref, bf16[512,2048]{1,0:T(8,128)(2,1)} %refs_0_.1, bf16[512,2048]{1,0:T(8,128)(2,1)} %copy-done, bf16[2048,4096]{1,0:T(8,128)(2,1)} %w_ref.3, bf16[2048,4096]{1,0:T(8,128)(2,1)} %w_ref.3, ...), custom_call_target="tpu_custom_call" | custom-call | tf_op jit(solution)/shard_map/grad_projection/pallas_call | solution.py:358
  86.1 14.0 %exchange_back.1 = f32[16,16,128]{2,1,0:T(8,128)} custom-call(f32[16,16,128]{2,1,0:T(8,128)} %bitcast.34, f32[16,16,128]{2,1,0:T(8,128)} %get-tuple-element.30.rates_ref), custom_call_target="tpu_custom_call" | custom-call | tf_op jit(solution)/shard_map/exchange_back/pallas_call | solution.py:252
  100.1 2.4 %collective-permute-done.1.refs_1_ = bf16[512,2048]{1,0:T(8,128)(2,1)} collective-permute-done((bf16[512,2048]{1,0:T(8,128)(2,1)}, bf16[512,2048]{1,0:T(8,128)(2,1)}, u32[]{:S(2)}, u32[]{:S(2)}) %collective-permute-start.1) | collective-permute-done | bytes 2097184 | tf_op jit(solution)/shard_map/ppermute | solution.py:348
  102.5 14.8 %backward_scan.1 = (bf16[512,2048]{1,0:T(8,128)(2,1)}, bf16[512,2048]{1,0:T(8,128)(2,1)}, bf16[512,2048]{1,0:T(8,128)(2,1)}) custom-call(bf16[512,2048]{1,0:T(8,128)(2,1)} %get-tuple-element.22.g_ref, bf16[512,2048]{1,0:T(8,128)(2,1)} %k_ref.5, bf16[512,2048]{1,0:T(8,128)(2,1)} %v_ref.5, f32[256,128]{1,0:T(8,128)} %bitcast.29, f32[256,128]{1,0:T(8,128)} %bitcast.31, ...), custom_call_target="tpu_custom_call" | custom-call | tf_op jit(solution)/shard_map/backward_scan/pallas_call | solution.py:376
Async XLA Ops:
  0.6 54.0 %collective-permute-start = (bf16[512,2048]{1,0:T(8,128)(2,1)}, bf16[512,2048]{1,0:T(8,128)(2,1)S(1)}, u32[]{:S(2)}, u32[]{:S(2)}) collective-permute-start(bf16[512,2048]{1,0:T(8,128)(2,1)} %refs_0_.1), channel_id=1, source_target_pairs={{1,0},{0,1},{3,2},{2,3},{5,4},{4,5},{7,6},{6,7},{9,8},{8,9},{11,10... | collective-permute-start | bytes 6291464 | tf_op jit(solution)/shard_map/ppermute | solution.py:276
  5.3 25.7 %copy-start.1 = (f32[2048,16]{0,1:T(8,128)S(1)}, f32[2048,16]{0,1:T(8,128)}, u32[]{:S(2)}) copy-start(f32[2048,16]{0,1:T(8,128)} %param.13) | copy-start | bytes 393220
  5.3 25.7 %copy-start.2 = (f32[2048,16]{0,1:T(8,128)S(1)}, f32[2048,16]{0,1:T(8,128)}, u32[]{:S(2)}) copy-start(f32[2048,16]{0,1:T(8,128)} %param.14) | copy-start | bytes 393220
  54.7 9.5 %copy-start = (bf16[512,2048]{1,0:T(8,128)(2,1)}, bf16[512,2048]{1,0:T(8,128)(2,1)S(1)}, u32[]{:S(2)}) copy-start(bf16[512,2048]{1,0:T(8,128)(2,1)S(1)} %collective-permute-done.refs_1_) | copy-start | bytes 6291460
  54.7 47.9 %collective-permute-start.1 = (bf16[512,2048]{1,0:T(8,128)(2,1)}, bf16[512,2048]{1,0:T(8,128)(2,1)}, u32[]{:S(2)}, u32[]{:S(2)}) collective-permute-start(bf16[512,2048]{1,0:T(8,128)(2,1)} %project.2), channel_id=1, source_target_pairs={{0,1},{1,0},{2,3},{3,2},{4,5},{5,4},{6,7},{7,6},{8,9},{9,8},{10,11... | collective-permute-start | bytes 6291464 | tf_op jit(solution)/shard_map/ppermute | solution.py:348
